TPU v7x, 256 devices: a whole 4x4x8 slice. The times are simulated.
256 devices in a mesh: ctx: 32 (over y, z), head: 8 (over x, core).
Axes of the slice: x: 4, y: 4, z: 8, core: 2. Of those that a mesh axis runs over, the one named last changes fastest.
Arguments:
- exponential_probe_vectors: bfloat16 [16384, 4096], P('ctx', 'head'), may hold values from -10 to 10
- exponential_lookup_vectors: bfloat16 [16384, 1024], P('ctx', 'head'), may hold values from -10 to 10
- exponential_content_vectors: bfloat16 [16384, 1024], P('ctx', 'head'), may hold values from -4 to 4
- linear_mixer_probe_vectors: bfloat16 [16384, 4096], P('ctx', 'head'), may hold values from -512 to 512
- linear_mixer_lookup_vectors: bfloat16 [16384, 4096], P('ctx', 'head'), may hold values from -4 to 4
- fading_powers: int32 [32], P('head'), may hold values from 5 to 19
- shrink_positions: int32 [16384], P('ctx'), may hold values 0 or 1
- final_rescale_weights: bfloat16 [4096], P('head'), may hold values from 0.099609375 to 1.8984375
Outputs:
- lightning_out: bfloat16 [16384, 4096], P('ctx', 'head')
All inputs are finite; a program needn't handle non-finite values. No bound on the sum of `shrink_positions` on one device may be relied on, other than what follows from the above.
Results may differ from a plain program's by a relative error of at most 0.023.
Values may be sent and summed in bfloat16 or wider, within the bound.
A program may use at most 64 MiB of HBM per device.

v0:
```python
import math

import jax
import jax.numpy as jnp
from jax import lax
from jax.sharding import PartitionSpec as P

HQ = 32
HD = 128


norm_epsilon = 1e-06
key_block = 1024


def from_behind(block, axis, distance):
    devices = range(lax.axis_size(axis))
    route = [(i - distance, i) for i in devices if i - distance in devices]
    return lax.ppermute(block, axis, route)


def sequence_position(row_index, span_rows, block_count):
    device_block = row_index // (2 * span_rows)
    offset_in = row_index % (2 * span_rows)
    return jnp.where(
        offset_in < span_rows,
        device_block * span_rows + offset_in,
        (block_count - 1 - device_block) * span_rows + offset_in - span_rows,
    )


def chain_combine(earlier, later):
    return (earlier[0] + later[0], jnp.exp(later[0])[:, None, None] * earlier[1] + later[1])


def choose_tuple(flag, former, latter):
    return jax.tree.map(
        lambda first_leaf, second_leaf: jnp.where(flag, first_leaf, second_leaf), former, latter
    )


def per_device(
    exponential_probe_vectors,
    exponential_lookup_vectors,
    exponential_content_vectors,
    linear_mixer_probe_vectors,
    linear_mixer_lookup_vectors,
    fading_powers,
    shrink_positions,
    final_rescale_weights,
):
    row_count = exponential_probe_vectors.shape[0]
    span_rows = row_count // 2
    devices = lax.axis_size("ctx")
    block_count = 2 * devices
    kv_local = exponential_lookup_vectors.shape[1] // HD
    heads_local = exponential_probe_vectors.shape[1] // HD
    group_size = heads_local // kv_local
    device_index = lax.axis_index("ctx")
    local_rows = device_index * row_count + jnp.arange(row_count, dtype=jnp.int32)
    query_pos = sequence_position(local_rows, span_rows, block_count)
    query_heads = exponential_probe_vectors.reshape(row_count, kv_local, group_size, HD)
    scaling = 1.0 / math.sqrt(HD)

    def key_step(carry, key_piece, value_piece, piece_start):
        highest, totals, accum = carry
        piece_rows = key_piece.shape[0]
        key_pos = sequence_position(
            piece_start + jnp.arange(piece_rows, dtype=jnp.int32), span_rows, block_count
        )
        scores = (
            jnp.einsum(
                "bhgd,shd->bhgs",
                query_heads,
                key_piece.reshape(piece_rows, kv_local, HD),
                preferred_element_type=jnp.float32,
            )
            * scaling
        )
        visible = key_pos[None, None, None, :] <= query_pos[:, None, None, None]
        raised = jnp.maximum(highest, jnp.max(jnp.where(visible, scores, -jnp.inf), axis=3))
        weights = jnp.where(visible, jnp.exp(scores - raised[..., None]), 0.0)
        factor = jnp.exp(highest - raised)
        totals = totals * factor + jnp.sum(weights, axis=3)
        accum = accum * factor[..., None] + jnp.einsum(
            "bhgs,shd->bhgd",
            weights.astype(jnp.bfloat16),
            value_piece.reshape(piece_rows, kv_local, HD),
            preferred_element_type=jnp.float32,
        )
        return (raised, totals, accum)

    start_carry = (
        jnp.full((row_count, kv_local, group_size), -1e30, jnp.float32),
        jnp.zeros((row_count, kv_local, group_size), jnp.float32),
        jnp.zeros((row_count, kv_local, group_size, HD), jnp.float32),
    )
    key_piece = lax.all_gather(exponential_lookup_vectors, "ctx", axis=0, tiled=True)
    value_piece = lax.all_gather(exponential_content_vectors, "ctx", axis=0, tiled=True)
    piece_rows = key_piece.shape[0]

    def inner_step(step_index, inner_carry):
        offset = step_index * key_block
        return key_step(
            inner_carry,
            lax.dynamic_slice_in_dim(key_piece, offset, key_block, 0),
            lax.dynamic_slice_in_dim(value_piece, offset, key_block, 0),
            offset,
        )

    highest, totals, accum = lax.fori_loop(0, piece_rows // key_block, inner_step, start_carry)
    exponential_weighted_mixer = (
        (accum / totals[..., None]).reshape(row_count, heads_local * HD).astype(jnp.bfloat16)
    )
    query_local = linear_mixer_probe_vectors.reshape(2, span_rows, heads_local, HD)
    key_local = linear_mixer_lookup_vectors.reshape(2, span_rows, heads_local, HD)
    value_local = exponential_weighted_mixer.reshape(2, span_rows, heads_local, HD)
    fading_speeds = jnp.exp2(-fading_powers.astype(jnp.float32))
    stride_natural_log = (
        -fading_speeds[None, :] - 0.5 * shrink_positions.astype(jnp.float32)[:, None]
    ).reshape(2, span_rows, heads_local)
    running = jnp.cumsum(stride_natural_log, axis=1)
    final_log = running[:, -1]
    lower = (jnp.arange(span_rows)[:, None] >= jnp.arange(span_rows)[None, :])[None, None]
    scores = jnp.einsum(
        "cthd,cshd->chts", query_local, key_local, preferred_element_type=jnp.float32
    )
    along = jnp.transpose(running, (0, 2, 1))
    distance = along[:, :, :, None] - along[:, :, None, :]
    decayed = jnp.where(lower, scores * jnp.exp(jnp.where(lower, distance, 0.0)), 0.0).astype(
        jnp.bfloat16
    )
    intra = jnp.einsum("chts,cshd->cthd", decayed, value_local, preferred_element_type=jnp.float32)
    scaled_keys = (
        key_local.astype(jnp.float32) * jnp.exp(final_log[:, None, :] - running)[..., None]
    )
    updates = jnp.einsum(
        "cthd,cthe->chde",
        scaled_keys,
        value_local.astype(jnp.float32),
        precision=lax.Precision.HIGHEST,
    )
    own_first = (final_log[0], updates[0])
    own_second = (final_log[1], updates[1])
    identity = (
        jnp.zeros((heads_local,), jnp.float32),
        jnp.zeros((heads_local, HD, HD), jnp.float32),
    )

    def forward_turn(turn_index, incoming):
        combined = chain_combine(incoming, own_first)
        return (
            from_behind(combined[0].astype(jnp.bfloat16), "ctx", 1).astype(jnp.float32),
            from_behind(combined[1].astype(jnp.bfloat16), "ctx", 1).astype(jnp.float32),
        )

    first_in = lax.fori_loop(0, devices - 1, forward_turn, identity)
    at_end = device_index == devices - 1
    seed_state = choose_tuple(at_end, chain_combine(first_in, own_first), identity)

    def backward_turn(turn_index, incoming):
        combined = chain_combine(incoming, own_second)
        moved = (
            from_behind(combined[0].astype(jnp.bfloat16), "ctx", -1).astype(jnp.float32),
            from_behind(combined[1].astype(jnp.bfloat16), "ctx", -1).astype(jnp.float32),
        )
        return choose_tuple(at_end, seed_state, moved)

    second_in = lax.fori_loop(0, devices - 1, backward_turn, seed_state)
    states = jnp.stack([first_in[1], second_in[1]])
    inter = jnp.einsum(
        "cthd,chde->cthe",
        query_local.astype(jnp.float32) * jnp.exp(running)[..., None],
        states,
        precision=lax.Precision.HIGHEST,
    )
    combined_result = (intra + inter).reshape(row_count, heads_local * HD)
    square_sum = lax.psum(jnp.sum(combined_result * combined_result, axis=1), "head")
    normed = (
        combined_result
        * lax.rsqrt(square_sum / (HQ * HD) + norm_epsilon)[:, None]
        * final_rescale_weights.astype(jnp.float32)[None, :]
    )
    return normed.astype(jnp.bfloat16)


def solution(mesh):
    placed = (
        P("ctx", "head"),
        P("ctx", "head"),
        P("ctx", "head"),
        P("ctx", "head"),
        P("ctx", "head"),
        P("head"),
        P("ctx"),
        P("head"),
    )
    return jax.shard_map(
        per_device, mesh=mesh, in_specs=placed, out_specs=P("ctx", "head"), check_vma=False
    )
```

profile of v0, /device:TPU:1, one launch (start us, length us, event | category | flops | bytes accessed | tf_op | source)
XLA Modules:
  0.0 982.9 jit_solution(12186463435217693812)
XLA Ops:
  18.6 75.0 %all-gather.5.cloned.1.call-done = bf16[16384,128]{0,1:T(8,128)(2,1)} async-done(((bf16[512,128]{0,1:T(8,128)(2,1)}), bf16[16384,128]{0,1:T(8,128)(2,1)}) %all-gather.5.cloned.1.call-update) | async-done | bytes 4194320 | tf_op jit(solution)/shard_map/all_gather | solution.py:99
  93.6 85.2 %all-gather.3.cloned.1.call-done = bf16[16384,128]{1,0:T(8,128)(2,1)} async-done(((bf16[512,128]{1,0:T(8,128)(2,1)}), bf16[16384,128]{1,0:T(8,128)(2,1)}) %all-gather.3.cloned.1.call-update) | async-done | bytes 4194320 | tf_op jit(solution)/shard_map/all_gather | solution.py:98
  178.9 220.7 %while.46 = (s32[]{:T(128)}, f32[512,1,4]{0,2,1:T(4,128)S(1)}, f32[512,1,4]{0,2,1:T(4,128)S(1)}, f32[512,1,4,128]{0,3,2,1:T(8,128)S(1)}, bf16[16384,128]{1,0:T(8...) while((s32[]{:T(128)}, f32[512,1,4]{0,2,1:T(4,128)S(1)}, ...), condition=%wide.region_3.4_spmd.clone, body=%wide.region_0.3_spmd.clone.sunk | while | flops 1098176512 | bytes 64106712 | solution.py:111
  184.9 5.8 fusion.81
  253.9 5.8 fusion.81
  401.0 228.7 %while.47 = (s32[]{:T(128)}, f32[4,128,128]{2,1,0:T(8,128)S(1)}, f32[4,1,1]{0,2,1:T(1,128)S(1)}, f32[4,128,128]{2,1,0:T(8,128)S(1)}, s32[]{:T(128)}, /*index=5*/s32[]{:T(128)}) while((s32[]{:T(128)}, f32[4,128,128]{2,1,0:T(8,128)S(1)}, f32[4,1,1]{0,2,1:T(1,128)S(1)}, f32[4,128,128]{2,1,0:T(8,128)S(1)}, s32[]{:T(128)}, ...), condition=%wide.region_7.8_spmd.clone, body=%wide.region_6.7_spmd.clone.sunk | while | flops 327683 | bytes 1572999 | solution.py:157
  443.2 6.0 collective-permute-start.1
  531.6 6.1 collective-permute-start.1
  539.8 6.0 collective-permute-start.1
  547.8 6.0 collective-permute-start.1
  555.9 6.2 collective-permute-start.1
  564.2 6.1 collective-permute-start.1
  573.4 6.5 collective-permute-start.1
  590.3 6.0 collective-permute-start.1
  598.3 5.9 collective-permute-start.1
  621.6 6.2 collective-permute-start.1
  630.0 260.2 %while.45 = (s32[]{:T(128)}, f32[4,128,128]{2,1,0:T(8,128)S(1)}, pred[]{:T(512)}, f32[4,1,1]{0,2,1:T(1,128)S(1)}, f32[4,128,128]{2,1,0:T(8,128)S(1)}, /*index=5*/f32[4,128,128]{2,1,0:T(8,128)S(1)}, s32[]{:T(128)}) while((s32[]{:T(128)}, f32[4,128,128]{2,1,0:T(8,128)S(1)}, pred[]{:T(512)}, f32[4,1,1]{0,2,1:T(1,128)S(1)}, ...), condition=%wide.region_9.10_spmd, body=%wide.region_8.9_spmd.sunk | while | flops 327682 | bytes 1835142 | solution.py:169
  631.5 7.0 collective-permute-done
  639.9 7.2 collective-permute-done
  648.5 7.2 collective-permute-done
  657.2 7.2 collective-permute-done
  665.9 7.6 collective-permute-done
  675.0 7.2 collective-permute-done
  683.6 7.0 collective-permute-done
  692.1 7.3 collective-permute-done
  700.8 6.5 collective-permute-done
  708.8 6.5 collective-permute-done
  716.8 8.6 collective-permute-done
  726.8 7.2 collective-permute-done
  735.5 6.9 collective-permute-done
  743.8 6.1 collective-permute-done
  751.4 6.7 collective-permute-done
  766.7 6.6 collective-permute-done
  774.7 8.1 collective-permute-done
  784.2 8.2 collective-permute-done
  793.8 6.4 collective-permute-done
  801.6 6.7 collective-permute-done
  809.8 7.0 collective-permute-done
  818.3 5.8 collective-permute-done
  825.5 5.8 collective-permute-done
  832.8 6.1 collective-permute-done
  840.4 7.6 collective-permute-done
  849.4 8.5 collective-permute-done
  859.3 6.9 collective-permute-done
  867.7 6.1 collective-permute-done
  875.3 7.0 collective-permute-done
  883.7 6.5 collective-permute-done
  895.2 79.9 %psum.7 = f32[512]{0:T(512)S(1)} all-reduce(f32[512]{0:T(512)S(1)} %bitcast.135), channel_id=1, replica_groups=mesh['ctx'=32,'head'=8] {'head'}, use_global_device_ids=true, to_apply=%region_11.12 | all-reduce | flops 512 | bytes 4096 | tf_op jit(solution)/shard_map/psum | solution.py:178
  (427 shorter events, 444.0 us)
Async XLA Ops:
  6.5 87.1 %all-gather.5.cloned.1.call-start = ((), (), s32[]{:S(2)}) async-start(), calls=%async_computation.1 | async-start | bytes 4325376 | tf_op jit(solution)/shard_map/all_gather | solution.py:99
  8.2 170.6 %all-gather.3.cloned.1.call-start = ((), (), s32[]{:S(2)}) async-start(), calls=%async_computation | async-start | bytes 4325376 | tf_op jit(solution)/shard_map/all_gather | solution.py:98
  443.2 7.9 collective-permute-start.1
  458.1 7.3 collective-permute-start.1
  479.6 7.8 collective-permute-start.1
  487.5 8.3 collective-permute-start.1
  509.8 7.3 collective-permute-start.1
  517.2 7.3 collective-permute-start.1
  531.6 8.0 collective-permute-start.1
  539.8 7.9 collective-permute-start.1
  547.8 7.9 collective-permute-start.1
  555.9 8.2 collective-permute-start.1
  564.2 9.1 collective-permute-start.1
  573.4 8.9 collective-permute-start.1
  582.5 7.6 collective-permute-start.1
  590.3 7.9 collective-permute-start.1
  598.3 7.9 collective-permute-start.1
  606.3 7.6 collective-permute-start.1
  614.1 7.3 collective-permute-start.1
  621.6 8.2 collective-permute-start.1
  630.2 8.3 collective-permute-start
  638.6 8.5 collective-permute-start
  647.2 8.5 collective-permute-start
  655.9 8.5 collective-permute-start
  664.6 8.9 collective-permute-start
  673.7 8.5 collective-permute-start
  682.3 8.3 collective-permute-start
  690.8 8.6 collective-permute-start
  699.5 7.8 collective-permute-start
  707.5 7.8 collective-permute-start
  715.5 9.9 %collective-permute-start = (bf16[4,128,128]{2,1,0:T(8,128)(2,1)S(1)}, bf16[4,128,128]{2,1,0:T(8,128)(2,1)S(1)}, u32[]{:S(2)}, u32[]{:S(2)}) collective-permute-start(bf16[4,128,128]{2,1,0:T(8,128)(2,1)S(1)} %add_convert_fusion.2), channel_id=1, source_target_pairs={{8,0},{16,8},{24,16},{32,24},{40,32},{48,40},{56,48},{64,56},{72,6... | collective-permute-start | bytes 393224 | tf_op jit(solution)/shard_map/while/body/eval_jaxpr/ppermute | solution.py:19
  725.5 8.5 collective-permute-start
  734.2 8.2 collective-permute-start
  742.5 7.4 collective-permute-start
  750.1 8.0 collective-permute-start
  765.4 7.9 collective-permute-start
  773.4 9.4 collective-permute-start
  782.9 9.5 collective-permute-start
  792.5 7.7 collective-permute-start
  800.3 8.0 collective-permute-start
  808.5 8.3 collective-permute-start
  831.5 7.4 collective-permute-start
  839.1 8.9 collective-permute-start
  848.1 9.8 collective-permute-start
  858.0 8.2 collective-permute-start
  866.4 7.4 collective-permute-start
  874.0 8.3 collective-permute-start
  882.4 7.8 collective-permute-start
  (32 other events, 196.8 us)
Sparse Core Ops, SparseCore 0:
  9.8 83.7 all-gather.4
  96.2 82.5 all-gather.2
where the time goes:
time: 1000 us; the launch traced here: 983 us
  waiting for transfers between devices  441 us (44%)
  starting transfers between devices  199 us (20%)
  matrix products  187 us (19%)
  blocking collectives  79.9 us (8%)
  other arithmetic  49.5 us (5%)
  between operations  13.6 us (1%)
    ppermute x62, waiting for transfers between devices, from_behind(): return lax.ppermute(block, axis, route)  280 us
    ppermute x62, starting transfers between devices, from_behind(): return lax.ppermute(block, axis, route)  199 us
    dot_general x16, matrix products, key_step(): jnp.einsum('bhgs,shd->bhgd', weights.astype(jnp.bfloat16), value_piece.re...  92.3 us
    dot_general x16, matrix products, key_step(): jnp.einsum('bhgd,shd->bhgs', query_heads, key_piece.reshape(piece_rows, k...  90.5 us
    all_gather x1, waiting for transfers between devices, per_device(): lax.all_gather(exponential_lookup_vectors, 'ctx', axis=0, tiled=True)  85.2 us
    psum x1, blocking collectives, per_device(): lax.psum(jnp.sum(combined_result * combined_result, axis=1), 'head')  79.9 us
    all_gather x1, waiting for transfers between devices, per_device(): lax.all_gather(exponential_content_vectors, 'ctx', axis=0, tiled=True)  75 us
    reduce_sum x16, other arithmetic, key_step(): totals = totals * factor + jnp.sum(weights, axis=3)  29.2 us
  transfers between devices with their start and end apart: 64, of which 64 were waited for; matrix products, arithmetic and copies ran while one was open for 1% of the time, Pallas kernels for 0%

commit v1 on v0

v1 whole, which is shorter than its diff:
```python
import functools
import math

import jax
import jax.numpy as jnp
from jax import lax
from jax.experimental import pallas as pl
from jax.experimental.pallas import tpu as pltpu
from jax.sharding import PartitionSpec as P

HQ = 32
HD = 128
SPAN = 256
HEADS = 4
ROWS_Y = 4
RING = 8
CTX = 32
GROUP = 8
NORM_EPSILON = 1e-06
LOW = -1e30
MESH = pl.DeviceIdType.MESH
F32 = jnp.float32
BF16 = jnp.bfloat16
NT = (((1,), (1,)), ((), ()))
NN = (((1,), (0,)), ((), ()))
TN = (((0,), (0,)), ((), ()))


def dot(a, b, dims=NN):
    return lax.dot_general(a, b, dims, preferred_element_type=F32)


def eye_mask():
    return lax.broadcasted_iota(jnp.int32, (128, 128), 0) == lax.broadcasted_iota(
        jnp.int32, (128, 128), 1
    )


def column_to_row(column):
    return jnp.sum(jnp.where(eye_mask(), column, 0.0), axis=0, keepdims=True)


def row_to_column(row):
    spread = jnp.where(eye_mask(), jnp.broadcast_to(row, (128, 128)), 0.0)
    return jnp.broadcast_to(jnp.sum(spread, axis=1, keepdims=True), (128, 128))


def twice(x):
    return jnp.concatenate([x, x], axis=1)


def split_queries(source, target):
    scale = math.log2(math.e) / math.sqrt(HD)
    for h in range(HEADS):
        scaled = source[:, h * HD : (h + 1) * HD].astype(F32) * scale
        high = scaled.astype(BF16)
        low = (scaled - high.astype(F32)).astype(BF16)
        target[h * SPAN : (h + 1) * SPAN, 0:HD] = high
        target[h * SPAN : (h + 1) * SPAN, HD : 2 * HD] = low


def attend(queries, keys, values, size, accum, highest, scores, masked=False):
    def product(h, slot):
        k = twice(keys[...].reshape(size, HD))
        s = dot(queries[h * SPAN : (h + 1) * SPAN, :], k, NT)
        if masked:
            row = lax.broadcasted_iota(jnp.int32, (SPAN, size), 0)
            col = lax.broadcasted_iota(jnp.int32, (SPAN, size), 1)
            s = jnp.where(col <= row, s, LOW)
        scores[slot, :, 0:size] = s

    def fold(h, slot):
        rows = slice(h * SPAN, (h + 1) * SPAN)
        s = scores[slot, :, 0:size]
        old = highest[rows, :]
        new = jnp.maximum(
            old, jnp.broadcast_to(jnp.max(s, axis=1, keepdims=True), (SPAN, HD))
        )
        factor = jnp.exp2(old - new)
        p = jnp.exp2(s - jnp.concatenate([new] * (size // HD), axis=1)).astype(BF16)
        v = values[...].reshape(size, HD)
        v = jnp.concatenate([v, jnp.ones_like(v)], axis=1)
        accum[rows, :] = accum[rows, :] * twice(factor) + dot(p, v)
        highest[rows, :] = new

    product(0, 0)
    for h in range(HEADS):
        if h + 1 < HEADS:
            product(h + 1, (h + 1) % 2)
        fold(h, h % 2)


def attention_kernel(
    q_ref, k_ref, v_ref, out_ref,
    qbuf, kbuf, vbuf, qs, accum, highest, scores, osend, lsend, orecv, lrecv,
    qsend_sem, qrecv_sem, kvsend_sem, kvrecv_sem, osend_sem, orecv_sem, lsend_sem, lrecv_sem,
):
    me = lax.axis_index("ctx")
    y, z = me // RING, lax.rem(me, RING)
    right = y * RING + lax.rem(z + 1, RING)
    left = y * RING + lax.rem(z + RING - 1, RING)

    def row_of(r):
        return lax.rem(y + r, ROWS_Y)

    def partner(r):
        return row_of(r) * RING + z

    barrier = pltpu.get_barrier_semaphore()
    for other in (left, right, partner(1), partner(2), partner(3)):
        pl.semaphore_signal(barrier, inc=1, device_id={"ctx": other}, device_id_type=MESH)
    pl.semaphore_wait(barrier, 5)

    def ring_copy(half, way, piece, s):
        buf, own = (kbuf, k_ref) if piece == 0 else (vbuf, v_ref)
        target = 1 if s == 3 else 2 * (s + 1) + way
        src = own.at[half] if s == 0 else buf.at[half, 2 * s + way]
        return pltpu.make_async_remote_copy(
            src_ref=src,
            dst_ref=buf.at[half, target],
            send_sem=kvsend_sem.at[half, way, piece, s],
            recv_sem=kvrecv_sem.at[half, way, piece, s],
            device_id={"ctx": right if way == 0 else left},
            device_id_type=MESH,
        )

    def pieces(way, s):
        return (0, 1) if s < 3 else (way,)

    def ring_send(half, s):
        for piece in (0, 1):
            for way in (0, 1):
                if piece in pieces(way, s):
                    ring_copy(half, way, piece, s).start()

    def ring_step(half, s):
        for piece in (0, 1):
            for way in (0, 1):
                if piece in pieces(way, s - 1):
                    ring_copy(half, way, piece, s - 1).wait_recv()
                if s < 4 and piece in pieces(way, s):
                    ring_copy(half, way, piece, s).start()

    def query_copy(r, half):
        return pltpu.make_async_remote_copy(
            src_ref=q_ref.at[half],
            dst_ref=qbuf.at[ROWS_Y - r, half],
            send_sem=qsend_sem.at[r, half],
            recv_sem=qrecv_sem.at[ROWS_Y - r, half],
            device_id={"ctx": partner(r)},
            device_id_type=MESH,
        )

    def query_arrival(r, half):
        return pltpu.make_async_remote_copy(
            src_ref=q_ref.at[half],
            dst_ref=qbuf.at[r, half],
            send_sem=qsend_sem.at[r, half],
            recv_sem=qrecv_sem.at[r, half],
            device_id={"ctx": partner(r)},
            device_id_type=MESH,
        )

    def result_copies(r, half, back):
        slot = r if back else ROWS_Y - r
        return (
            pltpu.make_async_remote_copy(
                src_ref=osend.at[r, half],
                dst_ref=orecv.at[slot, half],
                send_sem=osend_sem.at[r, half],
                recv_sem=orecv_sem.at[slot, half],
                device_id={"ctx": partner(r)},
                device_id_type=MESH,
            ),
            pltpu.make_async_remote_copy(
                src_ref=lsend.at[r, half],
                dst_ref=lrecv.at[slot, half],
                send_sem=lsend_sem.at[r, half],
                recv_sem=lrecv_sem.at[slot, half],
                device_id={"ctx": partner(r)},
                device_id_type=MESH,
            ),
        )

    ring_send(0, 0)
    for r in (3, 1, 2):

        @pl.when(y > row_of(r))
        def _(r=r):
            query_copy(r, 0).start()

        query_copy(r, 1).start()

    def clear(a):
        accum[a] = jnp.zeros((HEADS * SPAN, 2 * HD), F32)
        highest[a] = jnp.full((HEADS * SPAN, HD), LOW, F32)

    def single(half, slot, masked=False):
        attend(
            qs.at[half], kbuf.at[half, slot], vbuf.at[half, slot], SPAN,
            accum.at[half], highest.at[half], scores, masked,
        )

    kbuf[0, 0] = k_ref[0]
    vbuf[0, 0] = v_ref[0]
    kbuf[1, 0] = k_ref[1]
    vbuf[1, 0] = v_ref[1]
    for half in (0, 1):
        split_queries(q_ref.at[half], qs.at[half])
        clear(half)
        single(half, 0, masked=True)

    def pair(s):
        attend(
            qs.at[1], kbuf.at[0, 2 * s : 2 * s + 2], vbuf.at[0, 2 * s : 2 * s + 2], 2 * SPAN,
            accum.at[1], highest.at[1], scores,
        )

    for s in (1, 2, 3):
        ring_step(0, s)
        if s == 2:
            ring_send(1, 0)
        pair(s)

        @pl.loop(0, 2)
        def _(way, s=s):
            @pl.when(lax.rem(z + RING - s + 2 * s * way, RING) < z)
            def _():
                single(0, 2 * s + way)

    ring_step(0, 4)
    pair(0)

    @pl.when(z >= 4)
    def _():
        single(0, 1)

    def stream(slot, half, a):
        @pl.loop(0, 2)
        def _(c):
            attend(
                qs.at[slot], kbuf.at[half, pl.ds(4 * c, 4)], vbuf.at[half, pl.ds(4 * c, 4)],
                4 * SPAN, accum.at[a], highest.at[a], scores,
            )

    def emit(r, half, a):
        for h in range(HEADS):
            rows = slice(h * SPAN, (h + 1) * SPAN)
            total = accum[a, rows, HD : 2 * HD]
            osend[r, half, :, h * HD : (h + 1) * HD] = (accum[a, rows, 0:HD] / total).astype(BF16)
            level = highest[a, rows, :] + jnp.log2(total)
            for g in range(2):
                lsend[r, half, 2 * h + g : 2 * h + g + 1, :] = column_to_row(
                    level[g * 128 : (g + 1) * 128, :]
                )
        for copy in result_copies(r, half, False):
            copy.start()

    for turn, r in enumerate((3, 1, 2)):
        above = row_of(r) > y

        @pl.when(above)
        def _(r=r):
            query_arrival(r, 0).wait_recv()

        query_arrival(r, 1).wait_recv()
        split_queries(qbuf.at[r, jnp.where(above, 0, 1)], qs.at[2])
        clear(1 + r)
        stream(2, 0, 1 + r)

        @pl.when(above)
        def _(r=r):
            emit(r, 0, 1 + r)

        ring_step(1, turn + 1)

    ring_step(1, 4)

    for r in (3, 1, 2):
        above = row_of(r) > y

        @pl.when(above)
        def _(r=r):
            clear(1 + r)

        split_queries(qbuf.at[r, 1], qs.at[2])
        stream(2, jnp.where(above, 0, 1), 1 + r)
        emit(r, 1, 1 + r)

    @pl.loop(1, RING)
    def _(slot):
        s = slot // 2
        away = jnp.where(slot == 1, 4, jnp.where(lax.rem(slot, 2) == 0, RING - s, s))

        @pl.when(lax.rem(z + away, RING) > z)
        def _():
            single(1, slot)

    def combine(half):
        for r in (1, 2, 3):
            if half == 1:
                for copy in result_copies(r, 1, True):
                    copy.wait_recv()
            else:
                below = row_of(r) < y

                @pl.when(below)
                def _(r=r):
                    for copy in result_copies(r, 0, True):
                        copy.wait_recv()

                @pl.when(jnp.logical_not(below))
                def _(r=r):
                    orecv[r, 0] = jnp.zeros((SPAN, HEADS * HD), BF16)
                    lrecv[r, 0] = jnp.full((8, 128), LOW, F32)

        for h in range(HEADS):
            for g in range(2):
                rows = slice(h * SPAN + g * 128, h * SPAN + (g + 1) * 128)
                part = slice(g * 128, (g + 1) * 128)
                cols = slice(h * HD, (h + 1) * HD)
                total = accum[half, rows, HD : 2 * HD]
                levels = [highest[half, rows, :] + jnp.log2(total)]
                values = [accum[half, rows, 0:HD] / total]
                for r in (1, 2, 3):
                    levels.append(row_to_column(lrecv[r, half, 2 * h + g : 2 * h + g + 1, :]))
                    values.append(orecv[r, half, part, cols].astype(F32))
                top = functools.reduce(jnp.maximum, levels)
                weights = [jnp.exp2(level - top) for level in levels]
                mixed = sum(w * v for w, v in zip(weights, values)) / sum(weights)
                out_ref[half, part, cols] = mixed.astype(BF16)

    combine(0)
    combine(1)

    for half in (0, 1):
        for s in range(4):
            for way in (0, 1):
                for piece in pieces(way, s):
                    ring_copy(half, way, piece, s).wait_send()
    for r in (1, 2, 3):

        @pl.when(y > row_of(r))
        def _(r=r):
            query_copy(r, 0).wait_send()

        query_copy(r, 1).wait_send()

        @pl.when(row_of(r) > y)
        def _(r=r):
            for copy in result_copies(r, 0, False):
                copy.wait_send()

        for copy in result_copies(r, 1, False):
            copy.wait_send()


def lightning_kernel(
    a_ref, q_ref, k_ref, shrink_ref, fading_ref, gain_ref, out_ref,
    usend, urecv, ssend, srecv, mixed, qd, sqsend, sqrecv,
    usend_sem, urecv_sem, ssend_sem, srecv_sem, sqsend_sem, sqrecv_sem,
):
    me = lax.axis_index("ctx")
    head = lax.axis_index("head")

    barrier = pltpu.get_barrier_semaphore()

    @pl.loop(1, CTX)
    def _(k):
        pl.semaphore_signal(
            barrier, inc=1, device_id={"ctx": lax.rem(me + k, CTX)}, device_id_type=MESH
        )

    @pl.loop(1, GROUP)
    def _(k):
        pl.semaphore_signal(
            barrier, inc=1, device_id={"head": lax.rem(head + k, GROUP)}, device_id_type=MESH
        )

    row = lax.broadcasted_iota(jnp.int32, (SPAN, SPAN), 0)
    col = lax.broadcasted_iota(jnp.int32, (SPAN, SPAN), 1)
    lower = col <= row
    step_col = (lax.broadcasted_iota(jnp.int32, (SPAN, HD), 0) + 1).astype(F32)
    step_row = (lax.broadcasted_iota(jnp.int32, (8, SPAN), 1) + 1).astype(F32)
    for c in (0, 1):
        shrink = shrink_ref[c : c + 1, :].astype(F32)
        counts_col = jnp.broadcast_to(
            jnp.sum(jnp.where(lower, jnp.broadcast_to(shrink, (SPAN, SPAN)), 0.0), axis=1, keepdims=True),
            (SPAN, HD),
        )
        counts_row = dot(
            jnp.broadcast_to(shrink, (8, SPAN)).astype(BF16),
            jnp.where(row <= col, 1.0, 0.0).astype(BF16),
        )
        count = jnp.broadcast_to(jnp.sum(shrink, axis=1, keepdims=True), (16, HD))
        for h in range(HEADS):
            cols = slice(h * HD, (h + 1) * HD)
            power = fading_ref[h].astype(F32)
            speed_col = jnp.exp2(jnp.full((SPAN, HD), -power, F32))
            speed_row = jnp.exp2(jnp.full((8, SPAN), -power, F32))
            run_col = -speed_col * step_col - 0.5 * counts_col
            run_row = -speed_row * step_row - 0.5 * counts_row
            last = run_col[SPAN - 1 : SPAN, :]
            q = q_ref[c, :, cols]
            k = k_ref[c, :, cols]
            a = a_ref[c, :, cols]
            gap = jnp.minimum(twice(run_col) - jnp.broadcast_to(run_row[0:1, :], (SPAN, SPAN)), 0.0)
            decayed = jnp.where(lower, dot(q, k, NT) * jnp.exp(gap), 0.0).astype(BF16)
            mixed[c, :, cols] = dot(decayed, a)
            qd[c, :, cols] = (q.astype(F32) * jnp.exp(run_col)).astype(BF16)
            kd = (k.astype(F32) * jnp.exp(last - run_col)).astype(BF16)
            update = dot(kd, a, TN).astype(BF16)
            for part in range(8):
                usend[c, 8 * h + part, 0:16, :] = update[16 * part : 16 * (part + 1), :]
                usend[c, 8 * h + part, 16:32, :] = count.astype(BF16)

    pl.semaphore_wait(barrier, CTX - 1 + GROUP - 1)

    def update_copy(k):
        other = lax.rem(me + k, CTX)
        return pltpu.make_async_remote_copy(
            src_ref=usend.at[:, other],
            dst_ref=urecv.at[:, me],
            send_sem=usend_sem,
            recv_sem=urecv_sem,
            device_id={"ctx": other},
            device_id_type=MESH,
        )

    def update_all():
        return pltpu.make_async_remote_copy(
            src_ref=usend.at[:, 0 : CTX - 1],
            dst_ref=urecv.at[:, 0 : CTX - 1],
            send_sem=usend_sem,
            recv_sem=urecv_sem,
            device_id={"ctx": lax.rem(me + 1, CTX)},
            device_id_type=MESH,
        )

    def state_copy(k):
        other = lax.rem(me + k, CTX)
        return pltpu.make_async_remote_copy(
            src_ref=ssend.at[:, other],
            dst_ref=srecv.at[:, me],
            send_sem=ssend_sem,
            recv_sem=srecv_sem,
            device_id={"ctx": other},
            device_id_type=MESH,
        )

    def state_all():
        return pltpu.make_async_remote_copy(
            src_ref=ssend.at[:, 0 : CTX - 1],
            dst_ref=srecv.at[:, 0 : CTX - 1],
            send_sem=ssend_sem,
            recv_sem=srecv_sem,
            device_id={"ctx": lax.rem(me + 1, CTX)},
            device_id_type=MESH,
        )

    @pl.loop(1, CTX)
    def _(k):
        update_copy(k).start()

    for c in (0, 1):
        urecv[c, me] = usend[c, me]
    update_all().wait_recv()

    block_step = SPAN * jnp.exp2(jnp.full((16, HD), -fading_ref[me // 8].astype(F32), F32))
    state = jnp.zeros((16, HD), F32)
    for c, b in [(0, b) for b in range(CTX)] + [(1, b) for b in reversed(range(CTX))]:
        ssend[c, b] = state.astype(BF16)
        message = urecv[c, b].astype(F32)
        state = jnp.exp(-block_step - 0.5 * message[16:32, :]) * state + message[0:16, :]

    @pl.loop(1, CTX)
    def _(k):
        state_copy(k).start()

    for c in (0, 1):
        srecv[c, me] = ssend[c, me]
    state_all().wait_recv()

    for c in (0, 1):
        squares = jnp.zeros((SPAN, HD), F32)
        for h in range(HEADS):
            cols = slice(h * HD, (h + 1) * HD)
            state_h = srecv[c, 8 * h : 8 * h + 8].reshape(HD, HD)
            value = mixed[c, :, cols] + dot(qd[c, :, cols], state_h)
            mixed[c, :, cols] = value
            squares = squares + value * value
        column = jnp.broadcast_to(jnp.sum(squares, axis=1, keepdims=True), (SPAN, HD))
        for g in range(2):
            sqsend[2 * c + g : 2 * c + g + 1, :] = column_to_row(column[g * 128 : (g + 1) * 128, :])
    sqsend[4:8, :] = jnp.zeros((4, 128), F32)

    def square_copy(k):
        other = lax.rem(head + k, GROUP)
        return pltpu.make_async_remote_copy(
            src_ref=sqsend,
            dst_ref=sqrecv.at[GROUP - k],
            send_sem=sqsend_sem.at[k],
            recv_sem=sqrecv_sem.at[GROUP - k],
            device_id={"head": other},
            device_id_type=MESH,
        )

    for k in range(1, GROUP):
        square_copy(k).start()
    total = sqsend[...]
    for k in range(1, GROUP):
        square_copy(k).wait_recv()
        total = total + sqrecv[GROUP - k]
    scale = lax.rsqrt(total * (1.0 / (HQ * HD)) + NORM_EPSILON)
    for c in (0, 1):
        for g in range(2):
            column = row_to_column(scale[2 * c + g : 2 * c + g + 1, :])
            part = slice(g * 128, (g + 1) * 128)
            for h in range(HEADS):
                cols = slice(h * HD, (h + 1) * HD)
                gain = jnp.broadcast_to(gain_ref[0:1, cols].astype(F32), (128, HD))
                out_ref[c, part, cols] = (mixed[c, part, cols] * column * gain).astype(BF16)

    update_all().wait_send()
    state_all().wait_send()
    for k in range(1, GROUP):
        square_copy(k).wait_send()


VMEM = pl.BlockSpec(memory_space=pltpu.VMEM)
SMEM = pl.BlockSpec(memory_space=pltpu.SMEM)
WIDE = HEADS * HD


def per_device(q, k, v, lq, lk, fading, shrink, gain):
    dma = pltpu.SemaphoreType.DMA
    attention = pl.pallas_call(
        attention_kernel,
        out_shape=jax.ShapeDtypeStruct((2, SPAN, WIDE), BF16),
        in_specs=[VMEM] * 3,
        out_specs=VMEM,
        scratch_shapes=[
            pltpu.VMEM((ROWS_Y, 2, SPAN, WIDE), BF16),
            pltpu.VMEM((2, RING, SPAN, HD), BF16),
            pltpu.VMEM((2, RING, SPAN, HD), BF16),
            pltpu.VMEM((3, HEADS * SPAN, 2 * HD), BF16),
            pltpu.VMEM((5, HEADS * SPAN, 2 * HD), F32),
            pltpu.VMEM((5, HEADS * SPAN, HD), F32),
            pltpu.VMEM((2, SPAN, 4 * SPAN), F32),
            pltpu.VMEM((ROWS_Y, 2, SPAN, WIDE), BF16),
            pltpu.VMEM((ROWS_Y, 2, 8, 128), F32),
            pltpu.VMEM((ROWS_Y, 2, SPAN, WIDE), BF16),
            pltpu.VMEM((ROWS_Y, 2, 8, 128), F32),
            dma((ROWS_Y, 2)),
            dma((ROWS_Y, 2)),
            dma((2, 2, 2, 4)),
            dma((2, 2, 2, 4)),
            dma((ROWS_Y, 2)),
            dma((ROWS_Y, 2)),
            dma((ROWS_Y, 2)),
            dma((ROWS_Y, 2)),
        ],
        compiler_params=pltpu.CompilerParams(
            collective_id=0, has_side_effects=True, vmem_limit_bytes=48 * 2**20
        ),
    )(q.reshape(2, SPAN, WIDE), k.reshape(2, SPAN, HD), v.reshape(2, SPAN, HD))
    out = pl.pallas_call(
        lightning_kernel,
        out_shape=jax.ShapeDtypeStruct((2, SPAN, WIDE), BF16),
        in_specs=[VMEM, VMEM, VMEM, VMEM, SMEM, VMEM],
        out_specs=VMEM,
        scratch_shapes=[
            pltpu.VMEM((2, CTX, 32, HD), BF16),
            pltpu.VMEM((2, CTX, 32, HD), BF16),
            pltpu.VMEM((2, CTX, 16, HD), BF16),
            pltpu.VMEM((2, CTX, 16, HD), BF16),
            pltpu.VMEM((2, SPAN, WIDE), F32),
            pltpu.VMEM((2, SPAN, WIDE), BF16),
            pltpu.VMEM((8, 128), F32),
            pltpu.VMEM((GROUP, 8, 128), F32),
            dma,
            dma,
            dma,
            dma,
            dma((GROUP,)),
            dma((GROUP,)),
        ],
        compiler_params=pltpu.CompilerParams(
            collective_id=1, has_side_effects=True, vmem_limit_bytes=48 * 2**20
        ),
    )(
        attention,
        lq.reshape(2, SPAN, WIDE),
        lk.reshape(2, SPAN, WIDE),
        shrink.reshape(2, SPAN),
        fading,
        gain.reshape(1, WIDE),
    )
    return out.reshape(2 * SPAN, WIDE)


def solution(mesh):
    placed = (
        P("ctx", "head"),
        P("ctx", "head"),
        P("ctx", "head"),
        P("ctx", "head"),
        P("ctx", "head"),
        P("head"),
        P("ctx"),
        P("head"),
    )
    return jax.shard_map(
        per_device, mesh=mesh, in_specs=placed, out_specs=P("ctx", "head"), check_vma=False
    )
```

time: 1000 us -> 103 us (0.10); the launches traced: 983 us -> 103 us
  waiting for transfers between devices: 441 us -> 0 us
  starting transfers between devices: 199 us -> 0 us
  matrix products: 187 us -> 0 us
  Pallas kernels: 0 us -> 97.5 us
  blocking collectives: 79.9 us -> 0 us
  other arithmetic: 49.5 us -> 0 us
  between operations: 13.6 us -> 0.05 us
    ppermute x62 -> x0, waiting for transfers between devices: 280 us -> none  [from_behind(): return lax.ppermute(block, axis, route)]
    ppermute x62 -> x0, starting transfers between devices: 199 us -> none  [from_behind(): return lax.ppermute(block, axis, route)]
    dot_general x35 -> x0, matrix products: 187 us -> none  [the longest x16 92.3 us: key_step(): jnp.einsum('bhgs,shd->bhgd', weights.astype(jnp.bfloat16), value_piece.re...]
    all_gather x2 -> x0, waiting for transfers between devices: 160 us -> none  [the longest x1 85.2 us: per_device(): lax.all_gather(exponential_lookup_vectors, 'ctx', axis=0, tiled=True)]
    pallas_call x0 -> x2, Pallas kernels: none -> 97.5 us  [the longest x1 62.6 us: per_device(): pl.pallas_call(attention_kernel, out_shape=jax.ShapeDtypeStruct((2, SPAN,...]
    psum x1 -> x0, blocking collectives: 79.9 us -> none  [per_device(): lax.psum(jnp.sum(combined_result * combined_result, axis=1), 'head')]
    reduce_sum x16 -> x0, other arithmetic: 29.2 us -> none  [key_step(): totals = totals * factor + jnp.sum(weights, axis=3)]
  transfers between devices with their start and end apart: 64 -> 0, of which waited for: 64 -> 0; matrix products, arithmetic and copies ran while one was open for 1% -> 0% of each run, Pallas kernels for 0% -> 0%
where the time goes in v1:
time: 103 us
  Pallas kernels  97.5 us (95%)
  local copies, waits for them, and re-layouts  5.02 us (5%)
    pallas_call x1, Pallas kernels, per_device(): pl.pallas_call(attention_kernel, out_shape=jax.ShapeDtypeStruct((2, SPAN,...  62.6 us
    pallas_call x1, Pallas kernels, per_device(): pl.pallas_call(lightning_kernel, out_shape=jax.ShapeDtypeStruct((2, SPAN,...  34.9 us
    unnamed x17, local copies, waits for them, and re-layouts  5 us

profile of v1, /device:TPU:1, one launch (start us, length us, event | category | flops | bytes accessed | tf_op | source)
XLA Modules:
  0.0 102.6 jit_solution(4549003051270140679)
XLA Ops:
  0.0 0.0 copy-start.6
  0.0 0.7 copy-done.6
  0.7 0.0 copy-start.7
  0.7 0.7 copy-done.7
  1.4 0.0 copy-start.2
  1.4 1.0 %copy-done.2 = bf16[512,512]{1,0:T(8,128)(2,1)S(1)} copy-done((bf16[512,512]{1,0:T(8,128)(2,1)S(1)}, bf16[512,512]{1,0:T(8,128)(2,1)}, u32[]{:S(2)}) %copy-start.2) | copy-done | bytes 524312
  2.4 0.0 copy-start.3
  2.4 0.9 copy-done.3
  3.3 0.0 copy-start.4
  3.3 0.9 copy-done.4
  4.2 0.0 copy-start
  4.2 0.0 copy-start.1
  4.2 0.0 copy-start.5
  4.2 62.6 %shard_map.82.a_ref = bf16[2,256,512]{2,1,0:T(8,128)(2,1)S(1)} custom-call(bf16[2,256,512]{2,1,0:T(8,128)(2,1)S(1)} %bitcast.9, bf16[2,256,128]{2,1,0:T(8,128)(2,1)S(1)} %bitcast.10, bf16[2,256,128]{2,1,0:T(8,128)(2,1)S(1)} %bitcast.11), custom_call_target="tpu_custom_call" | custom-call | tf_op jit(solution)/shard_map/pallas_call | solution.py:537
  66.8 0.0 copy-done
  66.8 0.0 copy-done.1
  66.8 0.0 copy-done.5
  66.8 34.9 %shard_map.83 = bf16[2,256,512]{2,1,0:T(8,128)(2,1)S(1)} custom-call(bf16[2,256,512]{2,1,0:T(8,128)(2,1)S(1)} %shard_map.82.a_ref, bf16[2,256,512]{2,1,0:T(8,128)(2,1)S(1)} %bitcast.7, bf16[2,256,512]{2,1,0:T(8,128)(2,1)S(1)} %bitcast.8, s32[2,256]{1,0:T(2,128)S(1)} %reshape.29.shrink_ref, s32[4]{0:T(128)S(1)} %copy-done.5, bf16[1,512]{1,0:T(2,128)(2,1)S(1)} %reshape.30.gain_ref), custom_call_target="tpu_custom_call" | custom-call | tf_op jit(solution)/shard_map/pallas_call | solution.py:567
  101.8 0.8 copy.10
  (2 shorter events, 0.0 us)
Async XLA Ops:
  0.0 0.7 copy-start.6
  0.7 0.7 copy-start.7
  1.4 1.0 %copy-start.2 = (bf16[512,512]{1,0:T(8,128)(2,1)S(1)}, bf16[512,512]{1,0:T(8,128)(2,1)}, u32[]{:S(2)}) copy-start(bf16[512,512]{1,0:T(8,128)(2,1)} %param.8) | copy-start | bytes 1572868
  2.4 0.9 copy-start.3
  3.3 0.9 copy-start.4
  4.2 62.6 %copy-start = (bf16[512,512]{1,0:T(8,128)(2,1)S(1)}, bf16[512,512]{1,0:T(8,128)(2,1)}, u32[]{:S(2)}) copy-start(bf16[512,512]{1,0:T(8,128)(2,1)} %param.11) | copy-start | bytes 1572868
  4.2 62.6 %copy-start.1 = (bf16[512,512]{1,0:T(8,128)(2,1)S(1)}, bf16[512,512]{1,0:T(8,128)(2,1)}, u32[]{:S(2)}) copy-start(bf16[512,512]{1,0:T(8,128)(2,1)} %param.12) | copy-start | bytes 1572868
  4.2 62.6 %copy-start.5 = (s32[4]{0:T(128)S(1)}, s32[4]{0:T(128)}, u32[]{:S(2)}) copy-start(s32[4]{0:T(128)} %fading_ref.1) | copy-start | bytes 52

commit v2 on v1

v2 whole, which is shorter than its diff:
```python
import functools
import math

import jax
import jax.numpy as jnp
from jax import lax
from jax.experimental import pallas as pl
from jax.experimental.pallas import tpu as pltpu
from jax.sharding import PartitionSpec as P

HQ = 32
HD = 128
SPAN = 256
HEADS = 4
ROWS_Y = 4
RING = 8
CTX = 32
GROUP = 8
NORM_EPSILON = 1e-06
LOW = -1e30
MESH = pl.DeviceIdType.MESH
F32 = jnp.float32
BF16 = jnp.bfloat16
NT = (((1,), (1,)), ((), ()))
NN = (((1,), (0,)), ((), ()))
TN = (((0,), (0,)), ((), ()))


def dot(a, b, dims=NN):
    return lax.dot_general(a, b, dims, preferred_element_type=F32)


def eye_mask():
    return lax.broadcasted_iota(jnp.int32, (128, 128), 0) == lax.broadcasted_iota(
        jnp.int32, (128, 128), 1
    )


def column_to_row(column):
    return jnp.sum(jnp.where(eye_mask(), column, 0.0), axis=0, keepdims=True)


def row_to_column(row):
    spread = jnp.where(eye_mask(), jnp.broadcast_to(row, (128, 128)), 0.0)
    return jnp.broadcast_to(jnp.sum(spread, axis=1, keepdims=True), (128, 128))


def twice(x):
    return jnp.concatenate([x, x], axis=1)


def split_queries(source, target):
    scale = math.log2(math.e) / math.sqrt(HD)
    for h in range(HEADS):
        scaled = source[:, h * HD : (h + 1) * HD].astype(F32) * scale
        high = scaled.astype(BF16)
        low = (scaled - high.astype(F32)).astype(BF16)
        target[h * SPAN : (h + 1) * SPAN, 0:HD] = high
        target[h * SPAN : (h + 1) * SPAN, HD : 2 * HD] = low


def attend(items, scores):
    def product(item, h, slot):
        queries, keys, _, size, _, _, masked = item
        k = twice(keys[...].reshape(size, HD))
        s = dot(queries[h * SPAN : (h + 1) * SPAN, :], k, NT)
        if masked:
            row = lax.broadcasted_iota(jnp.int32, (SPAN, size), 0)
            col = lax.broadcasted_iota(jnp.int32, (SPAN, size), 1)
            s = jnp.where(col <= row, s, LOW)
        scores[slot, :, 0:size] = s

    def fold(item, h, slot):
        _, _, values, size, accum, highest, _ = item
        rows = slice(h * SPAN, (h + 1) * SPAN)
        s = scores[slot, :, 0:size]
        old = highest[rows, :]
        new = jnp.maximum(
            old, jnp.broadcast_to(jnp.max(s, axis=1, keepdims=True), (SPAN, HD))
        )
        factor = jnp.exp2(old - new)
        p = jnp.exp2(s - jnp.concatenate([new] * (size // HD), axis=1)).astype(BF16)
        v = values[...].reshape(size, HD)
        v = jnp.concatenate([v, jnp.ones_like(v)], axis=1)
        accum[rows, :] = accum[rows, :] * twice(factor) + dot(p, v)
        highest[rows, :] = new

    steps = [(item, h) for item in items for h in range(HEADS)]
    product(*steps[0], 0)
    for n, step in enumerate(steps):
        if n + 1 < len(steps):
            product(*steps[n + 1], (n + 1) % 2)
        fold(*step, n % 2)


def kernel(
    q_ref, k_ref, v_ref, lq_ref, lk_ref, shrink_ref, fading_ref, gain_ref, out_ref,
    qbuf, kbuf, vbuf, qs, accum, highest, scores, osend, lsend, orecv, lrecv,
    lq, lk, shrink_buf, mixer, decayed, kd, qd, mixed,
    decay, scan_state, usend, urecv, ssend, srecv, sqsend, sqrecv,
    load_sem, qsend_sem, qrecv_sem, kvsend_sem, kvrecv_sem, osend_sem, orecv_sem,
    lsend_sem, lrecv_sem, usend_sem, urecv_sem, ssend_sem, srecv_sem,
    sqsend_sem, sqrecv_sem,
):
    me = lax.axis_index("ctx")
    head = lax.axis_index("head")
    y, z = me // RING, lax.rem(me, RING)
    right = y * RING + lax.rem(z + 1, RING)
    left = y * RING + lax.rem(z + RING - 1, RING)

    def row_of(r):
        return lax.rem(y + r, ROWS_Y)

    def partner(r):
        return row_of(r) * RING + z

    loads = [
        pltpu.make_async_copy(source, target, load_sem.at[n])
        for n, (source, target) in enumerate(
            (
                (q_ref, qbuf.at[0]),
                (k_ref, kbuf.at[:, 0]),
                (v_ref, vbuf.at[:, 0]),
                (shrink_ref.at[pl.ds(0, SPAN)], shrink_buf.at[0]),
                (shrink_ref.at[pl.ds(SPAN, SPAN)], shrink_buf.at[1]),
                (lq_ref, lq),
                (lk_ref, lk),
            )
        )
    ]
    for load in loads:
        load.start()

    barrier = pltpu.get_barrier_semaphore()

    @pl.loop(1, CTX)
    def _(k):
        pl.semaphore_signal(
            barrier, inc=1, device_id={"ctx": lax.rem(me + k, CTX)}, device_id_type=MESH
        )

    @pl.loop(1, GROUP)
    def _(k):
        pl.semaphore_signal(
            barrier, inc=1, device_id={"head": lax.rem(head + k, GROUP)}, device_id_type=MESH
        )

    pl.semaphore_wait(barrier, CTX - 1 + GROUP - 1)

    def ring_copy(half, way, piece, s):
        buf, own = (kbuf, k_ref) if piece == 0 else (vbuf, v_ref)
        target = 1 if s == 3 else 2 * (s + 1) + way
        src = own.at[half] if s == 0 else buf.at[half, 2 * s + way]
        return pltpu.make_async_remote_copy(
            src_ref=src,
            dst_ref=buf.at[half, target],
            send_sem=kvsend_sem.at[half, way, piece, s],
            recv_sem=kvrecv_sem.at[half, way, piece, s],
            device_id={"ctx": right if way == 0 else left},
            device_id_type=MESH,
        )

    def pieces(way, s):
        return (0, 1) if s < 3 else (way,)

    def ring_send(half, s):
        for piece in (0, 1):
            for way in (0, 1):
                if piece in pieces(way, s):
                    ring_copy(half, way, piece, s).start()

    def ring_step(half, s):
        for piece in (0, 1):
            for way in (0, 1):
                if piece in pieces(way, s - 1):
                    ring_copy(half, way, piece, s - 1).wait_recv()
                if s < 4 and piece in pieces(way, s):
                    ring_copy(half, way, piece, s).start()

    def query_copy(r, half, slot=None):
        slot = ROWS_Y - r if slot is None else slot
        return pltpu.make_async_remote_copy(
            src_ref=q_ref.at[half],
            dst_ref=qbuf.at[slot, half],
            send_sem=qsend_sem.at[r, half],
            recv_sem=qrecv_sem.at[slot, half],
            device_id={"ctx": partner(r)},
            device_id_type=MESH,
        )

    def result_copies(r, half, slot=None):
        slot = ROWS_Y - r if slot is None else slot
        return (
            pltpu.make_async_remote_copy(
                src_ref=osend.at[r, half],
                dst_ref=orecv.at[slot, half],
                send_sem=osend_sem.at[r, half],
                recv_sem=orecv_sem.at[slot, half],
                device_id={"ctx": partner(r)},
                device_id_type=MESH,
            ),
            pltpu.make_async_remote_copy(
                src_ref=lsend.at[r, half],
                dst_ref=lrecv.at[slot, half],
                send_sem=lsend_sem.at[r, half],
                recv_sem=lrecv_sem.at[slot, half],
                device_id={"ctx": partner(r)},
                device_id_type=MESH,
            ),
        )

    def spread_copy(source, target, send_sem, recv_sem, k):
        other = lax.rem(me + k, CTX)
        return pltpu.make_async_remote_copy(
            src_ref=source(other),
            dst_ref=target(me),
            send_sem=send_sem,
            recv_sem=recv_sem,
            device_id={"ctx": other},
            device_id_type=MESH,
        )

    def spread_all(whole_source, whole_target, send_sem, recv_sem):
        return pltpu.make_async_remote_copy(
            src_ref=whole_source,
            dst_ref=whole_target,
            send_sem=send_sem,
            recv_sem=recv_sem,
            device_id={"ctx": lax.rem(me + 1, CTX)},
            device_id_type=MESH,
        )

    def message(c):
        return pl.ds(0, 32 if c == 0 else 16)

    def update_all(c):
        return spread_all(
            usend.at[c, 0 : CTX - 1, message(c)], urecv.at[c, 0 : CTX - 1, message(c)],
            usend_sem.at[c], urecv_sem.at[c],
        )

    def state_all(c):
        return spread_all(
            ssend.at[c, 0 : CTX - 1], srecv.at[c, 0 : CTX - 1], ssend_sem.at[c], srecv_sem.at[c]
        )

    def send_queries(r, stage):
        if stage == 0:

            @pl.when(y > row_of(r))
            def _():
                query_copy(r, 0).start()

            @pl.when(y < row_of(r))
            def _():
                query_copy(r, 1).start()

        else:

            @pl.when(y > row_of(r))
            def _():
                query_copy(r, 1).start()

    ring_send(0, 0)
    send_queries(3, 0)
    send_queries(1, 0)

    def clear(a):
        accum[a] = jnp.zeros((HEADS * SPAN, 2 * HD), F32)
        highest[a] = jnp.full((HEADS * SPAN, HD), LOW, F32)

    def single(half, slot, masked=False):
        return (
            qs.at[half], kbuf.at[half, slot], vbuf.at[half, slot], SPAN,
            accum.at[half], highest.at[half], masked,
        )

    def pair(a, s):
        return (
            qs.at[a], kbuf.at[0, 2 * s : 2 * s + 2], vbuf.at[0, 2 * s : 2 * s + 2], 2 * SPAN,
            accum.at[a], highest.at[a], False,
        )

    def prepare(c):
        row = lax.broadcasted_iota(jnp.int32, (SPAN, SPAN), 0)
        col = lax.broadcasted_iota(jnp.int32, (SPAN, SPAN), 1)
        lower = col <= row
        step_col = (lax.broadcasted_iota(jnp.int32, (SPAN, HD), 0) + 1).astype(F32)
        step_row = (lax.broadcasted_iota(jnp.int32, (8, SPAN), 1) + 1).astype(F32)
        shrink = shrink_buf[c : c + 1, :].astype(F32)
        counts_col = jnp.broadcast_to(
            jnp.sum(
                jnp.where(lower, jnp.broadcast_to(shrink, (SPAN, SPAN)), 0.0),
                axis=1, keepdims=True,
            ),
            (SPAN, HD),
        )
        counts_row = dot(
            jnp.broadcast_to(shrink, (8, SPAN)).astype(BF16),
            jnp.where(row <= col, 1.0, 0.0).astype(BF16),
        )
        for h in range(HEADS):
            cols = slice(h * HD, (h + 1) * HD)
            power = fading_ref[h].astype(F32)
            run_col = -jnp.exp2(jnp.full((SPAN, HD), -power, F32)) * step_col - 0.5 * counts_col
            run_row = -jnp.exp2(jnp.full((8, SPAN), -power, F32)) * step_row - 0.5 * counts_row
            last = run_col[SPAN - 1 : SPAN, :]
            q = lq[c, :, cols]
            k = lk[c, :, cols]
            gap = jnp.minimum(
                twice(run_col) - jnp.broadcast_to(run_row[0:1, :], (SPAN, SPAN)), 0.0
            )
            decayed[c, h] = jnp.where(lower, dot(q, k, NT) * jnp.exp(gap), 0.0).astype(BF16)
            qd[c, :, cols] = (q.astype(F32) * jnp.exp(run_col)).astype(BF16)
            kd[c, :, cols] = (k.astype(F32) * jnp.exp(last - run_col)).astype(BF16)

    def receive_queries(r):
        above = row_of(r) > y

        @pl.when(above)
        def _():
            query_copy(r, 0, r).wait_recv()

        @pl.when(jnp.logical_not(above))
        def _():
            query_copy(r, 1, r).wait_recv()

        split_queries(qbuf.at[r, jnp.where(above, 0, 1)], qs.at[1 + r])
        clear(1 + r)

    def stream(half, a):
        @pl.loop(0, 2)
        def _(c):
            item = (
                qs.at[a], kbuf.at[half, pl.ds(4 * c, 4)], vbuf.at[half, pl.ds(4 * c, 4)],
                4 * SPAN, accum.at[a], highest.at[a], False,
            )
            attend([item], scores)

    def emit(r, half):
        a = 1 + r
        for h in range(HEADS):
            rows = slice(h * SPAN, (h + 1) * SPAN)
            total = accum[a, rows, HD : 2 * HD]
            osend[r, half, :, h * HD : (h + 1) * HD] = (accum[a, rows, 0:HD] / total).astype(BF16)
            level = highest[a, rows, :] + jnp.log2(total)
            for g in range(2):
                lsend[r, half, 2 * h + g : 2 * h + g + 1, :] = column_to_row(
                    level[g * 128 : (g + 1) * 128, :]
                )
        for copy in result_copies(r, half):
            copy.start()

    def combine(half):
        for r in (1, 2, 3):
            if half == 1:
                for copy in result_copies(r, 1, r):
                    copy.wait_recv()
            else:
                below = row_of(r) < y

                @pl.when(below)
                def _(r=r):
                    for copy in result_copies(r, 0, r):
                        copy.wait_recv()

                @pl.when(jnp.logical_not(below))
                def _(r=r):
                    orecv[r, 0] = jnp.zeros((SPAN, HEADS * HD), BF16)
                    lrecv[r, 0] = jnp.full((8, 128), LOW, F32)

        for h in range(HEADS):
            for g in range(2):
                rows = slice(h * SPAN + g * 128, h * SPAN + (g + 1) * 128)
                part = slice(g * 128, (g + 1) * 128)
                cols = slice(h * HD, (h + 1) * HD)
                total = accum[half, rows, HD : 2 * HD]
                levels = [highest[half, rows, :] + jnp.log2(total)]
                values = [accum[half, rows, 0:HD] / total]
                for r in (1, 2, 3):
                    levels.append(row_to_column(lrecv[r, half, 2 * h + g : 2 * h + g + 1, :]))
                    values.append(orecv[r, half, part, cols].astype(F32))
                top = functools.reduce(jnp.maximum, levels)
                weights = [jnp.exp2(level - top) for level in levels]
                value = sum(w * v for w, v in zip(weights, values)) / sum(weights)
                mixer[half, part, cols] = value.astype(BF16)

    def send_updates(c):
        for h in range(HEADS):
            cols = slice(h * HD, (h + 1) * HD)
            update = dot(kd[c, :, cols], mixer[c, :, cols], TN).astype(BF16)
            usend[c, 8 * h : 8 * h + 8, 0:16] = update.reshape(8, 16, HD)
        if c == 0:
            counts = [
                jnp.broadcast_to(
                    jnp.sum(shrink_buf[n : n + 1, :].astype(F32), axis=1, keepdims=True), (8, HD)
                )
                for n in (0, 1)
            ]
            both = jnp.concatenate(counts, axis=0).astype(BF16)
            for n in range(CTX):
                usend[0, n, 16:32] = both

        @pl.loop(1, CTX)
        def _(k):
            spread_copy(
                lambda other: usend.at[c, other, message(c)],
                lambda mine: urecv.at[c, mine, message(c)],
                usend_sem.at[c], urecv_sem.at[c], k,
            ).start()

        urecv[c, me, message(c)] = usend[c, me, message(c)]
        for h in range(HEADS):
            cols = slice(h * HD, (h + 1) * HD)
            mixed[c, :, cols] = dot(decayed[c, h], mixer[c, :, cols])

    def scan(c):
        update_all(c).wait_recv()
        if c == 0:
            power = fading_ref[me // 8].astype(F32)
            block_step = SPAN * jnp.exp2(jnp.full((8, HD), -power, F32))
            for b in range(CTX):
                counts = urecv[0, b, 16:32].astype(F32)
                for n in (0, 1):
                    decay[n, b] = jnp.exp(-block_step - 0.5 * counts[8 * n : 8 * n + 8, :])
        state = jnp.zeros((16, HD), F32) if c == 0 else scan_state[...]
        for b in range(CTX) if c == 0 else reversed(range(CTX)):
            ssend[c, b] = state.astype(BF16)
            factor = decay[c, b]
            factor = jnp.concatenate([factor, factor], axis=0)
            state = factor * state + urecv[c, b, 0:16].astype(F32)
        if c == 0:
            scan_state[...] = state

        @pl.loop(1, CTX)
        def _(k):
            spread_copy(
                lambda other: ssend.at[c, other], lambda mine: srecv.at[c, mine],
                ssend_sem.at[c], srecv_sem.at[c], k,
            ).start()

        srecv[c, me] = ssend[c, me]

    def square_copy(c, k):
        return pltpu.make_async_remote_copy(
            src_ref=sqsend.at[c],
            dst_ref=sqrecv.at[c, GROUP - k],
            send_sem=sqsend_sem.at[c, k],
            recv_sem=sqrecv_sem.at[c, GROUP - k],
            device_id={"head": lax.rem(head + k, GROUP)},
            device_id_type=MESH,
        )

    def add_states(c):
        state_all(c).wait_recv()
        squares = jnp.zeros((SPAN, HD), F32)
        for h in range(HEADS):
            cols = slice(h * HD, (h + 1) * HD)
            state_h = srecv[c, 8 * h : 8 * h + 8].reshape(HD, HD)
            value = mixed[c, :, cols] + dot(qd[c, :, cols], state_h)
            mixed[c, :, cols] = value
            squares = squares + value * value
        column = jnp.broadcast_to(jnp.sum(squares, axis=1, keepdims=True), (SPAN, HD))
        sqsend[c] = jnp.zeros((8, 128), F32)
        for g in range(2):
            sqsend[c, g : g + 1, :] = column_to_row(column[g * 128 : (g + 1) * 128, :])
        for k in range(1, GROUP):
            square_copy(c, k).start()

    def finish(c):
        total = sqsend[c]
        for k in range(1, GROUP):
            square_copy(c, k).wait_recv()
        for k in range(1, GROUP):
            total = total + sqrecv[c, k]
        scale = lax.rsqrt(total * (1.0 / (HQ * HD)) + NORM_EPSILON)
        for g in range(2):
            column = row_to_column(scale[g : g + 1, :])
            part = slice(g * 128, (g + 1) * 128)
            for h in range(HEADS):
                cols = slice(h * HD, (h + 1) * HD)
                gain = jnp.broadcast_to(gain_ref[0:1, cols].astype(F32), (128, HD))
                out_ref[c, part, cols] = (mixed[c, part, cols] * column * gain).astype(BF16)

    def first_results(r):
        @pl.when(row_of(r) > y)
        def _():
            emit(r, 0)

    def second_job(r):
        above = row_of(r) > y

        @pl.when(above)
        def _():
            query_copy(r, 1, r).wait_recv()
            split_queries(qbuf.at[r, 1], qs.at[1 + r])
            clear(1 + r)

        stream(jnp.where(above, 0, 1), 1 + r)
        emit(r, 1)

    def singles(slots):
        items = []
        for slot in slots:
            away = 4 if slot == 1 else (RING - slot // 2 if slot % 2 == 0 else slot // 2)
            items.append(single(jnp.where(lax.rem(z + away, RING) < z, 0, 1), slot))
        return items

    for n in range(3):
        loads[n].wait()
    for half in (0, 1):
        split_queries(qbuf.at[0, half], qs.at[half])
        clear(half)
    attend([single(0, 0, True), single(1, 0, True)], scores)
    for n in range(3, len(loads)):
        loads[n].wait()
    prepare(0)
    ring_step(0, 1)
    send_queries(2, 0)
    attend([pair(1, 1)], scores)
    prepare(1)
    ring_step(0, 2)
    ring_send(1, 0)
    receive_queries(3)
    receive_queries(1)
    attend([pair(4, 1), pair(2, 1), pair(4, 2), pair(2, 2)], scores)
    ring_step(0, 3)
    for r in (1, 2, 3):
        send_queries(r, 1)
    attend([pair(4, 3), pair(2, 3), pair(1, 2)], scores)
    ring_step(0, 4)
    ring_step(1, 1)
    attend([pair(4, 0), pair(2, 0)], scores)
    first_results(3)
    first_results(1)
    ring_step(1, 2)
    receive_queries(2)
    stream(0, 3)
    first_results(2)
    ring_step(1, 3)
    for r in (1, 2):
        pl.when(y == ROWS_Y - r)(lambda: ring_step(1, 4))
        second_job(r)
    pl.when(y < 2)(lambda: ring_step(1, 4))
    attend(singles((2, 3, 4, 5, 6, 7, 1)), scores)
    combine(0)
    send_updates(0)
    second_job(3)
    attend([pair(1, 3), pair(1, 0)], scores)
    scan(0)
    combine(1)
    send_updates(1)
    add_states(0)
    scan(1)
    finish(0)
    add_states(1)
    finish(1)

    for half in (0, 1):
        for s in range(4):
            for way in (0, 1):
                for piece in pieces(way, s):
                    ring_copy(half, way, piece, s).wait_send()
    for r in (1, 2, 3):

        @pl.when(y > row_of(r))
        def _(r=r):
            query_copy(r, 0).wait_send()

        query_copy(r, 1).wait_send()

        @pl.when(row_of(r) > y)
        def _(r=r):
            for copy in result_copies(r, 0):
                copy.wait_send()

        for copy in result_copies(r, 1):
            copy.wait_send()
    for c in (0, 1):
        update_all(c).wait_send()
        state_all(c).wait_send()
        for k in range(1, GROUP):
            square_copy(c, k).wait_send()


WIDE = HEADS * HD


def per_device(q, k, v, lq, lk, fading, shrink, gain):
    dma = pltpu.SemaphoreType.DMA
    anywhere = pl.BlockSpec(memory_space=pl.ANY)
    vmem = pltpu.VMEM
    out = pl.pallas_call(
        kernel,
        out_shape=jax.ShapeDtypeStruct((2, SPAN, WIDE), BF16),
        in_specs=[anywhere] * 6
        + [pl.BlockSpec(memory_space=pltpu.SMEM), pl.BlockSpec(memory_space=pltpu.VMEM)],
        out_specs=pl.BlockSpec(memory_space=pltpu.VMEM),
        scratch_shapes=[
            vmem((ROWS_Y, 2, SPAN, WIDE), BF16),
            vmem((2, RING, SPAN, HD), BF16),
            vmem((2, RING, SPAN, HD), BF16),
            vmem((5, HEADS * SPAN, 2 * HD), BF16),
            vmem((5, HEADS * SPAN, 2 * HD), F32),
            vmem((5, HEADS * SPAN, HD), F32),
            vmem((2, SPAN, 4 * SPAN), F32),
            vmem((ROWS_Y, 2, SPAN, WIDE), BF16),
            vmem((ROWS_Y, 2, 8, 128), F32),
            vmem((ROWS_Y, 2, SPAN, WIDE), BF16),
            vmem((ROWS_Y, 2, 8, 128), F32),
            vmem((2, SPAN, WIDE), BF16),
            vmem((2, SPAN, WIDE), BF16),
            vmem((2, SPAN), jnp.int32),
            vmem((2, SPAN, WIDE), BF16),
            vmem((2, HEADS, SPAN, SPAN), BF16),
            vmem((2, SPAN, WIDE), BF16),
            vmem((2, SPAN, WIDE), BF16),
            vmem((2, SPAN, WIDE), F32),
            vmem((2, CTX, 8, HD), F32),
            vmem((16, HD), F32),
            vmem((2, CTX, 32, HD), BF16),
            vmem((2, CTX, 32, HD), BF16),
            vmem((2, CTX, 16, HD), BF16),
            vmem((2, CTX, 16, HD), BF16),
            vmem((2, 8, 128), F32),
            vmem((2, GROUP, 8, 128), F32),
            dma((7,)),
            dma((ROWS_Y, 2)),
            dma((ROWS_Y, 2)),
            dma((2, 2, 2, 4)),
            dma((2, 2, 2, 4)),
            dma((ROWS_Y, 2)),
            dma((ROWS_Y, 2)),
            dma((ROWS_Y, 2)),
            dma((ROWS_Y, 2)),
            dma((2,)),
            dma((2,)),
            dma((2,)),
            dma((2,)),
            dma((2, GROUP)),
            dma((2, GROUP)),
        ],
        compiler_params=pltpu.CompilerParams(
            collective_id=0, has_side_effects=True, vmem_limit_bytes=56 * 2**20
        ),
    )(
        q.reshape(2, SPAN, WIDE),
        k.reshape(2, SPAN, HD),
        v.reshape(2, SPAN, HD),
        lq.reshape(2, SPAN, WIDE),
        lk.reshape(2, SPAN, WIDE),
        shrink,
        fading,
        gain.reshape(1, WIDE),
    )
    return out.reshape(2 * SPAN, WIDE)


def solution(mesh):
    placed = (
        P("ctx", "head"),
        P("ctx", "head"),
        P("ctx", "head"),
        P("ctx", "head"),
        P("ctx", "head"),
        P("head"),
        P("ctx"),
        P("head"),
    )
    return jax.shard_map(
        per_device, mesh=mesh, in_specs=placed, out_specs=P("ctx", "head"), check_vma=False
    )
```

time: 103 us -> 85.5 us (0.83)
  Pallas kernels: 97.5 us -> 82.2 us
  local copies, waits for them, and re-layouts: 5.02 us -> 3.13 us
    pallas_call x2 -> x1, Pallas kernels: 97.5 us -> 82.2 us  [per_device(): pl.pallas_call(kernel, out_shape=jax.ShapeDtypeStruct((2, SPAN, WIDE), BF...]
    unnamed x17 -> x3, local copies, waits for them, and re-layouts: 5 us -> 2.55 us
where the time goes in v2:
time: 85.5 us; the launch traced here: 85.3 us
  Pallas kernels  82.2 us (96%)
  local copies, waits for them, and re-layouts  3.13 us (4%)
    pallas_call x1, Pallas kernels, per_device(): pl.pallas_call(kernel, out_shape=jax.ShapeDtypeStruct((2, SPAN, WIDE), BF...  82.2 us
    unnamed x3, local copies, waits for them, and re-layouts  2.55 us

profile of v2, /device:TPU:1, one launch (start us, length us, event | category | flops | bytes accessed | tf_op | source)
XLA Modules:
  0.0 85.3 jit_solution(2002725061943898960)
XLA Ops:
  0.0 0.0 copy-start
  0.0 0.7 copy-done
  0.7 0.6 reshape.26.gain_ref
  1.3 82.2 %shard_map.82 = bf16[2,256,512]{2,1,0:T(8,128)(2,1)} custom-call(bf16[2,256,512]{2,1,0:T(8,128)(2,1)} %bitcast.7, bf16[2,256,128]{2,1,0:T(8,128)(2,1)} %bitcast.10, bf16[2,256,128]{2,1,0:T(8,128)(2,1)} %bitcast.11, bf16[2,256,512]{2,1,0:T(8,128)(2,1)} %bitcast.8, bf16[2,256,512]{2,1,0:T(8,128)(2,1)} %bitcast.9, s32[512]{0:T(512)} %shrink_ref.1, ...), custom_call_target="tpu_custom_call" | custom-call | tf_op jit(solution)/shard_map/pallas_call | solution.py:593
  83.5 1.9 %copy.10 = bf16[512,512]{1,0:T(8,128)(2,1)} copy(bf16[512,512]{1,0:T(8,128)(2,1)} %bitcast.6) | data formatting | bytes 1048576
Async XLA Ops:
  0.0 0.7 copy-start

commit v3 on v2

--- a/solution.py
+++ b/solution.py
@@ -487,17 +487,19 @@
         def _():
             emit(r, 0)
 
-    def second_job(r):
-        above = row_of(r) > y
-
-        @pl.when(above)
+    def second_queries(r):
+        @pl.when(row_of(r) > y)
         def _():
             query_copy(r, 1, r).wait_recv()
             split_queries(qbuf.at[r, 1], qs.at[1 + r])
             clear(1 + r)
 
-        stream(jnp.where(above, 0, 1), 1 + r)
-        emit(r, 1)
+    def part(r, c):
+        half = jnp.where(row_of(r) > y, 0, 1)
+        return (
+            qs.at[1 + r], kbuf.at[half, 4 * c : 4 * c + 4], vbuf.at[half, 4 * c : 4 * c + 4],
+            4 * SPAN, accum.at[1 + r], highest.at[1 + r], False,
+        )
 
     def singles(slots):
         items = []
@@ -537,45 +539,54 @@
     receive_queries(2)
     stream(0, 3)
     first_results(2)
+    def drain():
+        for half in (0, 1):
+            for s in range(4):
+                for way in (0, 1):
+                    for piece in pieces(way, s):
+                        ring_copy(half, way, piece, s).wait_send()
+        for r in (1, 2, 3):
+
+            @pl.when(y > row_of(r))
+            def _(r=r):
+                query_copy(r, 0).wait_send()
+
+            query_copy(r, 1).wait_send()
+
+            @pl.when(row_of(r) > y)
+            def _(r=r):
+                for copy in result_copies(r, 0):
+                    copy.wait_send()
+
+            for copy in result_copies(r, 1):
+                copy.wait_send()
+
+    attend(singles((2, 3, 4, 5)), scores)
     ring_step(1, 3)
-    for r in (1, 2):
-        pl.when(y == ROWS_Y - r)(lambda: ring_step(1, 4))
-        second_job(r)
-    pl.when(y < 2)(lambda: ring_step(1, 4))
-    attend(singles((2, 3, 4, 5, 6, 7, 1)), scores)
+    second_queries(1)
+    second_queries(2)
+    attend([part(1, 1), part(2, 1)], scores)
+    ring_step(1, 4)
+    attend([part(1, 0)], scores)
+    emit(1, 1)
+    attend([part(2, 0)], scores)
+    emit(2, 1)
+    second_queries(3)
+    attend([part(3, 1), part(3, 0)], scores)
+    emit(3, 1)
+    attend(singles((6, 7, 1)) + [pair(1, 3), pair(1, 0)], scores)
     combine(0)
     send_updates(0)
-    second_job(3)
-    attend([pair(1, 3), pair(1, 0)], scores)
-    scan(0)
     combine(1)
     send_updates(1)
+    drain()
+    scan(0)
+    scan(1)
     add_states(0)
-    scan(1)
+    add_states(1)
     finish(0)
-    add_states(1)
     finish(1)
 
-    for half in (0, 1):
-        for s in range(4):
-            for way in (0, 1):
-                for piece in pieces(way, s):
-                    ring_copy(half, way, piece, s).wait_send()
-    for r in (1, 2, 3):
-
-        @pl.when(y > row_of(r))
-        def _(r=r):
-            query_copy(r, 0).wait_send()
-
-        query_copy(r, 1).wait_send()
-
-        @pl.when(row_of(r) > y)
-        def _(r=r):
-            for copy in result_copies(r, 0):
-                copy.wait_send()
-
-        for copy in result_copies(r, 1):
-            copy.wait_send()
     for c in (0, 1):
         update_all(c).wait_send()
         state_all(c).wait_send()

time: 85.5 us -> 84.6 us (0.989)
  Pallas kernels: 82.2 us -> 81.3 us
    pallas_call x1, Pallas kernels: 82.2 us -> 81.3 us  [per_device(): pl.pallas_call(kernel, out_shape=jax.ShapeDtypeStruct((2, SPAN, WIDE), BF...]
where the time goes in v3:
time: 84.6 us; the launch traced here: 84.4 us
  Pallas kernels  81.3 us (96%)
  local copies, waits for them, and re-layouts  3.13 us (4%)
    pallas_call x1, Pallas kernels, per_device(): pl.pallas_call(kernel, out_shape=jax.ShapeDtypeStruct((2, SPAN, WIDE), BF...  81.3 us
    unnamed x3, local copies, waits for them, and re-layouts  2.55 us

profile of v3, /device:TPU:1, one launch (start us, length us, event | category | flops | bytes accessed | tf_op | source)
XLA Modules:
  0.0 84.4 jit_solution(13896744742442094783)
XLA Ops:
  0.0 0.0 copy-start
  0.0 0.7 copy-done
  0.7 0.6 reshape.26.gain_ref
  1.3 81.3 %shard_map.82 = bf16[2,256,512]{2,1,0:T(8,128)(2,1)} custom-call(bf16[2,256,512]{2,1,0:T(8,128)(2,1)} %bitcast.7, bf16[2,256,128]{2,1,0:T(8,128)(2,1)} %bitcast.10, bf16[2,256,128]{2,1,0:T(8,128)(2,1)} %bitcast.11, bf16[2,256,512]{2,1,0:T(8,128)(2,1)} %bitcast.8, bf16[2,256,512]{2,1,0:T(8,128)(2,1)} %bitcast.9, s32[512]{0:T(512)} %shrink_ref.1, ...), custom_call_target="tpu_custom_call" | custom-call | tf_op jit(solution)/shard_map/pallas_call | solution.py:604
  82.5 1.9 %copy.10 = bf16[512,512]{1,0:T(8,128)(2,1)} copy(bf16[512,512]{1,0:T(8,128)(2,1)} %bitcast.6) | data formatting | bytes 1048576
Async XLA Ops:
  0.0 0.7 copy-start
